TPU v7x, 32 devices: a whole 2x2x4 slice. The times are simulated.
32 devices in a mesh: row: 8 (over z, y), col: 4 (over x, core).
Axes of the slice: x: 2, y: 2, z: 4, core: 2. Of those that a mesh axis runs over, the one named last changes fastest.
Arguments:
- attn_in: bfloat16 [256, 16384], P('row', 'col'), may hold values from -6 to 6
- w_out: bfloat16 [16384, 16384], P('col', 'row'), may hold values from -0.046875 to 0.046875
- resid: bfloat16 [256, 16384], P('col', 'row'), may hold values from -64 to 64, as said below
- norm_gain: float32 [16384], P('row'), may hold values from 0.1 to 1.9
- w_gate: bfloat16 [16384, 26624], P('row', 'col'), may hold values from -0.046875 to 0.046875
- w_up: bfloat16 [16384, 26624], P('row', 'col'), may hold values from -0.046875 to 0.046875
- w_down: bfloat16 [26624, 16384], P('col', 'row'), may hold values from -0.0390625 to 0.0390625
Outputs:
- layer_out: bfloat16 [256, 16384], P('col', 'row')
Inputs may be any that keep to these rules, and one draw needn't show every extreme that they name: `resid`: entries are real-valued and not all of one size.
All inputs are finite; a program needn't handle non-finite values.
Results may differ from a plain program's by a relative error of at most 0.0051.
Values may be sent and summed in bfloat16 or wider, within the bound.
A program may use at most 192 MiB of HBM per device.

v0:
```python
import jax
import jax.numpy as jnp
from jax import lax
from jax.sharding import PartitionSpec as P

D = 16384


epsilon = 1e-05


def on_device(attn_in, w_out, resid, norm_gain, w_gate, w_up, w_down):
    panels = lax.all_gather(attn_in, "row", axis=0, tiled=True)
    token_rows = panels
    projected = lax.psum_scatter(
        jnp.dot(token_rows, w_out, preferred_element_type=jnp.float32),
        "col",
        scatter_dimension=0,
        tiled=True,
    )
    stream = (resid.astype(jnp.float32) + projected).astype(jnp.bfloat16)
    stream_f = stream.astype(jnp.float32)
    partial_value = jnp.sum(stream_f * stream_f, axis=1)
    sum_squares = lax.psum(partial_value, "row")
    mean_square = sum_squares / D
    normed = (stream_f * lax.rsqrt(mean_square + epsilon)[:, None] * norm_gain[None, :]).astype(
        jnp.bfloat16
    )
    every_token = lax.all_gather(normed, "col", axis=0, tiled=True)
    hidden_width = w_gate.shape[1]
    summed = lax.psum_scatter(
        jnp.concatenate(
            [
                jnp.dot(every_token, w_gate, preferred_element_type=jnp.float32),
                jnp.dot(every_token, w_up, preferred_element_type=jnp.float32),
            ],
            axis=1,
        ),
        "row",
        scatter_dimension=0,
        tiled=True,
    )
    activated = (jax.nn.silu(summed[:, :hidden_width]) * summed[:, hidden_width:]).astype(
        jnp.bfloat16
    )
    act_all = lax.all_gather(activated, "row", axis=0, tiled=True)
    token_rows = act_all
    down = lax.psum_scatter(
        jnp.dot(token_rows, w_down, preferred_element_type=jnp.float32),
        "col",
        scatter_dimension=0,
        tiled=True,
    )
    return (stream_f + down).astype(jnp.bfloat16)


def solution(mesh):
    placed = (
        P("row", "col"),
        P("col", "row"),
        P("col", "row"),
        P("row"),
        P("row", "col"),
        P("row", "col"),
        P("col", "row"),
    )
    return jax.shard_map(
        on_device, mesh=mesh, in_specs=placed, out_specs=P("col", "row"), check_vma=False
    )
```

profile of v0, /device:TPU:1, one launch (start us, length us, event | category | flops | bytes accessed | tf_op | source)
XLA Modules:
  0.0 514.4 jit_solution(16745238454019692555)
XLA Ops:
  6.5 0.0 all-gather.4.cloned.1.call-start
  6.5 0.7 all-gather.4.cloned.1.call-update
  7.3 0.0 copy-start
  7.3 0.0 copy-start.1
  7.3 0.0 reduce-scatter.4.cloned.1.call-start
  7.3 52.5 %all-gather.4.cloned.1.call-done = bf16[256,4096]{1,0:T(8,128)(2,1)} async-done(((bf16[32,4096]{1,0:T(8,128)(2,1)}), bf16[256,4096]{1,0:T(8,128)(2,1)}) %all-gather.4.cloned.1.call-update) | async-done | bytes 2097168 | tf_op jit(solution)/shard_map/all_gather | solution.py:13
  59.8 12.2 %fusion.5 = f32[256,2048]{1,0:T(8,128)} fusion(bf16[256,4096]{1,0:T(8,128)(2,1)} %all-gather.4.cloned.1.call-done, bf16[4096,2048]{1,0:T(8,128)(2,1)} %param.8), kind=kOutput, calls=%fused_computation.12 | convolution fusion | flops 4294967296 | bytes 20971520 | tf_op jit(solution)/shard_map/dot_general | solution.py:16
  72.0 0.0 reduce-scatter.4.cloned.1.call-update
  72.0 0.0 all-gather.6.cloned.1.call-start
  72.1 31.1 %reduce-scatter.4.cloned.1.call-done = f32[64,2048]{1,0:T(8,128)} async-done(((f32[256,2048]{1,0:T(8,128)}), f32[64,2048]{1,0:T(8,128)}) %reduce-scatter.4.cloned.1.call-update) | async-done | bytes 524304 | tf_op jit(solution)/shard_map/reduce_scatter | solution.py:15
  103.2 0.0 copy-done
  103.2 1.2 fusion.1
  104.5 17.6 %psum.7 = f32[64]{0:T(128)S(1)} all-reduce(f32[64]{0:T(128)S(1)} %get-tuple-element.5), channel_id=1, replica_groups=mesh['row'=8,'col'=4] {'row'}, use_global_device_ids=true, to_apply=%region_2.0 | all-reduce | flops 64 | bytes 512 | tf_op jit(solution)/shard_map/psum | solution.py:24
  122.1 0.0 copy-done.1
  122.1 0.8 fusion.3
  122.9 0.0 all-gather.6.cloned.1.call-update
  122.9 0.0 reduce-scatter.6.cloned.1.call-start
  123.0 17.3 %all-gather.6.cloned.1.call-done = bf16[256,2048]{1,0:T(8,128)(2,1)} async-done(((bf16[64,2048]{1,0:T(8,128)(2,1)}), bf16[256,2048]{1,0:T(8,128)(2,1)}) %all-gather.6.cloned.1.call-update) | async-done | bytes 1048592 | tf_op jit(solution)/shard_map/all_gather | solution.py:29
  140.3 16.4 %fusion.7 = f32[256,6656]{1,0:T(8,128)S(1)} fusion(bf16[256,2048]{1,0:T(8,128)(2,1)} %all-gather.6.cloned.1.call-done, bf16[2048,6656]{1,0:T(8,128)(2,1)} %param.12), kind=kOutput, calls=%fused_computation.14 | convolution fusion | flops 6979321856 | bytes 35127296 | tf_op jit(solution)/shard_map/dot_general | solution.py:35
  156.7 12.5 %fusion.6 = f32[256,6656]{1,0:T(8,128)S(1)} fusion(bf16[256,2048]{1,0:T(8,128)(2,1)S(1)} %copy-done.2, bf16[2048,6656]{1,0:T(8,128)(2,1)} %param.11), kind=kOutput, calls=%fused_computation.13 | convolution fusion | flops 6979321856 | bytes 35127296 | tf_op jit(solution)/shard_map/dot_general | solution.py:34
  169.2 5.3 %pad_maximum_fusion = f32[256,13312]{1,0:T(8,128)} fusion(f32[256,6656]{1,0:T(8,128)S(1)} %fusion.7, f32[256,6656]{1,0:T(8,128)S(1)} %fusion.6), kind=kLoop, calls=%fused_computation | loop fusion | flops 3407872 | bytes 27262976 | tf_op jit(solution)/shard_map/concatenate | solution.py:32
  174.4 0.0 reduce-scatter.6.cloned.1.call-update
  174.4 0.0 all-gather.8.cloned.1.call-start
  174.5 221.6 %reduce-scatter.6.cloned.1.call-done = f32[32,13312]{1,0:T(8,128)} async-done(((f32[256,13312]{1,0:T(8,128)}), f32[32,13312]{1,0:T(8,128)}) %reduce-scatter.6.cloned.1.call-update) | async-done | bytes 1703952 | tf_op jit(solution)/shard_map/reduce_scatter | solution.py:31
  396.0 2.4 fusion
  398.4 0.0 all-gather.8.cloned.1.call-update
  398.5 0.2 reduce-scatter.8.cloned.1.call-start
  398.7 61.6 %all-gather.8.cloned.1.call-done = bf16[256,6656]{1,0:T(8,128)(2,1)} async-done(((bf16[32,6656]{1,0:T(8,128)(2,1)}), bf16[256,6656]{1,0:T(8,128)(2,1)}) %all-gather.8.cloned.1.call-update) | async-done | bytes 3407888 | tf_op jit(solution)/shard_map/all_gather | solution.py:46
  460.3 14.4 %fusion.8 = f32[256,2048]{1,0:T(8,128)} fusion(bf16[256,6656]{1,0:T(8,128)(2,1)} %all-gather.8.cloned.1.call-done, bf16[6656,2048]{1,0:T(8,128)(2,1)} %param.13), kind=kOutput, calls=%fused_computation.15 | convolution fusion | flops 6979321856 | bytes 32768000 | tf_op jit(solution)/shard_map/dot_general | solution.py:49
  474.7 0.0 reduce-scatter.8.cloned.1.call-update
  474.7 31.0 %reduce-scatter.8.cloned.1.call-done = f32[64,2048]{1,0:T(8,128)} async-done(((f32[256,2048]{1,0:T(8,128)}), f32[64,2048]{1,0:T(8,128)}) %reduce-scatter.8.cloned.1.call-update) | async-done | bytes 524304 | tf_op jit(solution)/shard_map/reduce_scatter | solution.py:48
  505.7 1.8 fusion.4
  (3 shorter events, 0.0 us)
Async XLA Ops:
  6.5 53.2 %all-gather.4.cloned.1.call-start = ((), (), s32[]{:S(2)}) async-start(), calls=%async_computation.3 | async-start | bytes 2359296 | tf_op jit(solution)/shard_map/all_gather | solution.py:13
  7.3 96.0 %copy-start = (bf16[64,2048]{1,0:T(8,128)(2,1)S(1)}, bf16[64,2048]{1,0:T(8,128)(2,1)}, u32[]{:S(2)}) copy-start(bf16[64,2048]{1,0:T(8,128)(2,1)} %param.9) | copy-start | bytes 786436
  7.3 114.8 %copy-start.1 = (f32[2048]{0:T(1024)S(1)}, f32[2048]{0:T(1024)}, u32[]{:S(2)}) copy-start(f32[2048]{0:T(1024)} %param.10) | copy-start | bytes 24580
  7.3 96.0 %reduce-scatter.4.cloned.1.call-start = ((), (), s32[]{:S(2)}) async-start(), calls=%async_computation.4 | async-start | bytes 2621440 | tf_op jit(solution)/shard_map/reduce_scatter | solution.py:15
  72.0 68.2 %all-gather.6.cloned.1.call-start = ((), (), s32[]{:S(2)}) async-start(), calls=%async_computation.5 | async-start | bytes 1310720 | tf_op jit(solution)/shard_map/all_gather | solution.py:29
  122.9 273.1 %reduce-scatter.6.cloned.1.call-start = ((), (), s32[]{:S(2)}) async-start(), calls=%async_computation.6 | async-start | bytes 15335424 | tf_op jit(solution)/shard_map/reduce_scatter | solution.py:31
  140.3 16.4 %copy-start.2 = (bf16[256,2048]{1,0:T(8,128)(2,1)S(1)}, bf16[256,2048]{1,0:T(8,128)(2,1)}, u32[]{:S(2)}) copy-start(bf16[256,2048]{1,0:T(8,128)(2,1)} %all-gather.6.cloned.1.call-done) | copy-start | bytes 3145732
  174.4 285.8 %all-gather.8.cloned.1.call-start = ((), (), s32[]{:S(2)}) async-start(), calls=%async_computation.7 | async-start | bytes 3833856 | tf_op jit(solution)/shard_map/all_gather | solution.py:46
  398.5 107.3 %reduce-scatter.8.cloned.1.call-start = ((), (), s32[]{:S(2)}) async-start(), calls=%async_computation.8 | async-start | bytes 2621440 | tf_op jit(solution)/shard_map/reduce_scatter | solution.py:48
Sparse Core Ops, SparseCore 0:
  9.5 50.2 all-gather.3
  72.2 31.0 reduce-scatter.3
  123.1 17.1 all-gather.5
  174.6 221.4 reduce-scatter.5
  398.6 61.6 all-gather.7
  474.8 30.8 reduce-scatter.7
where the time goes:
time: 515 us; the launch traced here: 514 us
  waiting for transfers between devices  416 us (81%)
  matrix products  55.5 us (11%)
  blocking collectives  17.6 us (3%)
  between operations  13.5 us (3%)
  other arithmetic  11.5 us (2%)
    reduce_scatter x1, waiting for transfers between devices, on_device(): lax.psum_scatter(jnp.concatenate([jnp.dot(every_token, w_gate, preferred_...  222 us
    all_gather x1, waiting for transfers between devices, on_device(): act_all = lax.all_gather(activated, 'row', axis=0, tiled=True)  61.6 us
    all_gather x1, waiting for transfers between devices, on_device(): panels = lax.all_gather(attn_in, 'row', axis=0, tiled=True)  52.5 us
    reduce_scatter x1, waiting for transfers between devices, on_device(): lax.psum_scatter(jnp.dot(token_rows, w_out, preferred_element_type=jnp.fl...  31.1 us
    reduce_scatter x1, waiting for transfers between devices, on_device(): lax.psum_scatter(jnp.dot(token_rows, w_down, preferred_element_type=jnp.f...  31 us
    psum x1, blocking collectives, on_device(): sum_squares = lax.psum(partial_value, 'row')  17.6 us
    all_gather x1, waiting for transfers between devices, on_device(): every_token = lax.all_gather(normed, 'col', axis=0, tiled=True)  17.3 us
    dot_general x1, matrix products, on_device(): jnp.dot(every_token, w_up, preferred_element_type=jnp.float32)  16.4 us
  transfers between devices with their start and end apart: 6, of which 6 were waited for; matrix products, arithmetic and copies ran while one was open for 0% of the time, Pallas kernels for 0%

commit v1 on v0

v1 whole, which is shorter than its diff:
```python
import functools

import jax
import jax.numpy as jnp
from jax import lax
from jax.experimental import pallas as pl
from jax.experimental.pallas import tpu as pltpu
from jax.sharding import PartitionSpec as P

MESH = pl.DeviceIdType.MESH
F32, BF16 = jnp.float32, jnp.bfloat16
epsilon = 1e-05
SLOTS = 3


def chunk_of(hidden):
    return max(c for c in range(128, 513, 128) if hidden % c == 0)


def grid_of(rows):
    inner = 1
    while (2 * inner) ** 2 <= rows:
        inner *= 2
    return rows // inner, inner


def layer_kernel(
    Z, Y, Q, T, C, NF, NC,
    attn, w_out, resid, gain, w_gate, w_up, w_down,
    out,
    wo_buf, wg_buf, wu_buf,
    feat, ysend, yrecv, zrecv, act,
    acc, normed, stream, dsend, drecv1, drecv2, sq_send, sq_recv,
    wo_sem, wg_sem, wu_sem, wd_sem,
    f_zs, f_zr, f_ys, f_yr,
    r_ys, r_yr, r_zs, r_zr,
    a_zs, a_zr, a_ys, a_yr,
    p_s, p_r, d_s, d_r, q_s, q_r, n_s, n_r,
):
    n = Z * Y
    row, col = lax.axis_index("row"), lax.axis_index("col")
    z, y = row // Y, lax.rem(row, Y)
    tokens, width = normed.shape
    TB = tokens // Q

    def z_peer(d):
        return lax.rem(z + d, Z)

    def y_peer(d):
        return lax.rem(y + d, Y)

    def to_row(src, dst, send, recv, peer):
        return pltpu.make_async_remote_copy(
            src_ref=src, dst_ref=dst, send_sem=send, recv_sem=recv,
            device_id={"row": peer}, device_id_type=MESH,
        )

    def to_col(src, dst, send, recv, peer):
        return pltpu.make_async_remote_copy(
            src_ref=src, dst_ref=dst, send_sem=send, recv_sem=recv,
            device_id={"col": peer}, device_id_type=MESH,
        )

    def columns(c):
        return pl.ds(pl.multiple_of(c * C, C), C)

    def load_wo(f):
        return pltpu.make_async_copy(w_out.at[columns(f)], wo_buf.at[f], wo_sem.at[f])

    def load_gu(c):
        s = lax.rem(c, SLOTS)
        return (
            pltpu.make_async_copy(w_gate.at[:, columns(c)], wg_buf.at[s], wg_sem.at[s]),
            pltpu.make_async_copy(w_up.at[:, columns(c)], wu_buf.at[s], wu_sem.at[s]),
        )

    def load_wd(c):
        s = lax.rem(c, NF)
        return pltpu.make_async_copy(w_down.at[columns(c)], wo_buf.at[s], wd_sem.at[s])

    @pl.loop(0, NF)
    def _(f):
        load_wo(f).start()

    @pl.loop(0, SLOTS)
    def _(c):
        for copy in load_gu(c):
            copy.start()

    barrier = pltpu.get_barrier_semaphore()
    for d in range(1, n):
        pl.semaphore_signal(barrier, inc=1, device_id={"row": lax.rem(row + d, n)}, device_id_type=MESH)
    for d in range(1, Q):
        pl.semaphore_signal(barrier, inc=1, device_id={"col": lax.rem(col + d, Q)}, device_id_type=MESH)
    pl.semaphore_wait(barrier, n - 1 + Q - 1)

    def gather_z(buf, c, zs, zr):
        return [
            to_row(buf.at[c, y, z], buf.at[c, y, z], zs.at[c, d - 1], zr.at[c, d - 1], z_peer(d) * Y + y)
            for d in range(1, Z)
        ]

    def gather_y(buf, c, ys, yr):
        return [
            to_row(buf.at[c, y], buf.at[c, y], ys.at[c, d - 1], yr.at[c, d - 1], z * Y + y_peer(d))
            for d in range(1, Y)
        ]

    def reduce_cols(recv, s_sem, r_sem):
        for r in range(n):
            at = ((r % Y) * Z + r // Y) * T
            dsend[r * T : (r + 1) * T] = acc[at : at + T].astype(BF16)
        copies = []
        for d in range(1, Q):
            peer = lax.rem(col + d, Q)
            copies.append(
                to_col(
                    dsend.at[pl.ds(pl.multiple_of(peer * TB, TB), TB)],
                    recv.at[d - 1], s_sem.at[d - 1], r_sem.at[d - 1], peer,
                )
            )
        for copy in copies:
            copy.start()
        total = dsend[pl.ds(pl.multiple_of(col * TB, TB), TB)].astype(F32)
        for copy in copies:
            copy.wait()
        for d in range(Q - 1):
            total = total + recv[d].astype(F32)
        return total

    for f in range(NF):
        feat[f, y, z] = attn[:, f * C : (f + 1) * C]
    acc[...] = jnp.zeros_like(acc)

    @pl.loop(0, NF)
    def _(f):
        for copy in gather_z(feat, f, f_zs, f_zr):
            copy.start()

    @pl.loop(0, NF + 1)
    def _(t):
        @pl.when(t < NF)
        def _():
            for copy in gather_z(feat, t, f_zs, f_zr):
                copy.wait_recv()
            for copy in gather_y(feat, t, f_ys, f_yr):
                copy.start()

        @pl.when(t >= 1)
        def _():
            f = t - 1
            for copy in gather_y(feat, f, f_ys, f_yr):
                copy.wait()
            for copy in gather_z(feat, f, f_zs, f_zr):
                copy.wait_send()
            load_wo(f).wait()
            acc[...] += jnp.dot(feat[f].reshape(tokens, C), wo_buf[f], preferred_element_type=F32)

    @pl.loop(0, min(NF, NC))
    def _(c):
        load_wd(c).start()

    stream_now = (resid[...].astype(F32) + reduce_cols(drecv1, p_s, p_r)).astype(BF16)
    stream[...] = stream_now
    stream_f = stream_now.astype(F32)

    sq_send[...] = jnp.broadcast_to(jnp.sum(stream_f * stream_f, axis=1, keepdims=True), sq_send.shape)
    copies = [
        to_row(sq_send, sq_recv.at[d - 1], q_s.at[d - 1], q_r.at[d - 1], lax.rem(row + d, n))
        for d in range(1, n)
    ]
    for copy in copies:
        copy.start()
    acc[...] = jnp.zeros_like(acc)
    for copy in copies:
        copy.wait()
    squares = sq_send[...]
    for d in range(n - 1):
        squares = squares + sq_recv[d]
    scale = lax.rsqrt(squares[:, :1] / (width * n) + epsilon)
    own = pl.ds(pl.multiple_of(col * TB, TB), TB)
    normed[own] = (stream[...].astype(F32) * scale * gain[...]).astype(BF16)
    copies = [
        to_col(normed.at[own], normed.at[own], n_s.at[d - 1], n_r.at[d - 1], lax.rem(col + d, Q))
        for d in range(1, Q)
    ]
    for copy in copies:
        copy.start()
    for copy in copies:
        copy.wait()

    def reduce_y(c):
        return [
            to_row(ysend.at[c, y_peer(d)], yrecv.at[c, d - 1], r_ys.at[c, d - 1], r_yr.at[c, d - 1], z * Y + y_peer(d))
            for d in range(1, Y)
        ]

    def reduce_z(c):
        return [
            to_row(ysend.at[c, y, z_peer(d)], zrecv.at[c, d - 1], r_zs.at[c, d - 1], r_zr.at[c, d - 1], z_peer(d) * Y + y)
            for d in range(1, Z)
        ]

    def multiply(c):
        s = lax.rem(c, SLOTS)
        gate_copy, up_copy = load_gu(c)
        for half, copy, buf in ((0, gate_copy, wg_buf), (1, up_copy, wu_buf)):
            copy.wait()
            part = jnp.dot(normed[...], buf[s], preferred_element_type=F32).astype(BF16)
            for r in range(n):
                ysend[c, r % Y, r // Y, :, half * C : (half + 1) * C] = part[r * T : (r + 1) * T]
        for copy in reduce_y(c):
            copy.start()

        @pl.when(c + SLOTS < NC)
        def _():
            for copy in load_gu(c + SLOTS):
                copy.start()

    def add_y(c):
        for copy in reduce_y(c):
            copy.wait_recv()
        total = ysend[c, y].astype(F32)
        for d in range(Y - 1):
            total = total + yrecv[c, d].astype(F32)
        ysend[c, y] = total.astype(BF16)
        for copy in reduce_z(c):
            copy.start()

    def activate(c):
        for copy in reduce_z(c):
            copy.wait_recv()
        total = ysend[c, y, z].astype(F32)
        for d in range(Z - 1):
            total = total + zrecv[c, d].astype(F32)
        gate, up = total[:, :C], total[:, C:]
        act[c, y, z] = (gate / (1.0 + jnp.exp(-gate)) * up).astype(BF16)
        for copy in gather_z(act, c, a_zs, a_zr):
            copy.start()

    def pass_on(c):
        for copy in gather_z(act, c, a_zs, a_zr):
            copy.wait_recv()
        for copy in gather_y(act, c, a_ys, a_yr):
            copy.start()

    def project_down(c):
        for copy in gather_y(act, c, a_ys, a_yr):
            copy.wait()
        for copy in gather_z(act, c, a_zs, a_zr) + reduce_y(c) + reduce_z(c):
            copy.wait_send()
        load_wd(c).wait()
        acc[...] += jnp.dot(act[c].reshape(tokens, C), wo_buf[lax.rem(c, NF)], preferred_element_type=F32)

        @pl.when(c + NF < NC)
        def _():
            load_wd(c + NF).start()

    stages = ((0, multiply), (2, add_y), (3, activate), (4, pass_on), (5, project_down))

    @pl.loop(0, NC + 5)
    def _(t):
        for lag, stage in stages:

            @pl.when((t >= lag) & (t < NC + lag))
            def _():
                stage(t - lag)

    out[...] = (stream[...].astype(F32) + reduce_cols(drecv2, d_s, d_r)).astype(out.dtype)


def on_device(Z, Y, Q, attn_in, w_out, resid, norm_gain, w_gate, w_up, w_down):
    n = Z * Y
    T, features = attn_in.shape
    width, hidden = w_gate.shape
    tokens = T * n
    TB = tokens // Q
    C = chunk_of(hidden)
    NF, NC = features // C, hidden // C
    dma = pltpu.SemaphoreType.DMA
    vmem, hbm = pl.BlockSpec(memory_space=pltpu.VMEM), pl.BlockSpec(memory_space=pl.ANY)

    def pairs(count, peers):
        return [dma((count, peers)), dma((count, peers))]

    def both(peers):
        return [dma((peers,)), dma((peers,))]

    return pl.pallas_call(
        functools.partial(layer_kernel, Z, Y, Q, T, C, NF, NC),
        out_shape=jax.ShapeDtypeStruct((TB, width), BF16),
        in_specs=[vmem, hbm, vmem, vmem, hbm, hbm, hbm],
        out_specs=vmem,
        scratch_shapes=[
            pltpu.VMEM((NF, C, width), BF16),
            pltpu.VMEM((SLOTS, width, C), BF16),
            pltpu.VMEM((SLOTS, width, C), BF16),
            pltpu.VMEM((NF, Y, Z, T, C), BF16),
            pltpu.VMEM((NC, Y, Z, T, 2 * C), BF16),
            pltpu.VMEM((NC, Y - 1, Z, T, 2 * C), BF16),
            pltpu.VMEM((NC, Z - 1, T, 2 * C), BF16),
            pltpu.VMEM((NC, Y, Z, T, C), BF16),
            pltpu.VMEM((tokens, width), F32),
            pltpu.VMEM((tokens, width), BF16),
            pltpu.VMEM((TB, width), BF16),
            pltpu.VMEM((tokens, width), BF16),
            pltpu.VMEM((Q - 1, TB, width), BF16),
            pltpu.VMEM((Q - 1, TB, width), BF16),
            pltpu.VMEM((TB, 128), F32),
            pltpu.VMEM((n - 1, TB, 128), F32),
            dma((NF,)), dma((SLOTS,)), dma((SLOTS,)), dma((NF,)),
            *pairs(NF, Z - 1), *pairs(NF, Y - 1),
            *pairs(NC, Y - 1), *pairs(NC, Z - 1),
            *pairs(NC, Z - 1), *pairs(NC, Y - 1),
            *both(Q - 1), *both(Q - 1), *both(n - 1), *both(Q - 1),
        ],
        compiler_params=pltpu.CompilerParams(
            collective_id=0, has_side_effects=True, vmem_limit_bytes=60 * 2**20
        ),
    )(attn_in, w_out, resid, norm_gain.reshape(1, width), w_gate, w_up, w_down)


def solution(mesh):
    Z, Y = grid_of(mesh.shape["row"])
    placed = (
        P("row", "col"),
        P("col", "row"),
        P("col", "row"),
        P("row"),
        P("row", "col"),
        P("row", "col"),
        P("col", "row"),
    )
    return jax.shard_map(
        functools.partial(on_device, Z, Y, mesh.shape["col"]),
        mesh=mesh, in_specs=placed, out_specs=P("col", "row"), check_vma=False,
    )
```

time: 515 us -> 213 us (0.41)
  waiting for transfers between devices: 416 us -> 0 us
  Pallas kernels: 0 us -> 212 us
  matrix products: 55.5 us -> 0 us
  blocking collectives: 17.6 us -> 0 us
  between operations: 13.5 us -> 0.01 us
  other arithmetic: 11.5 us -> 0 us
    reduce_scatter x3 -> x0, waiting for transfers between devices: 284 us -> none  [the longest x1 222 us: on_device(): lax.psum_scatter(jnp.concatenate([jnp.dot(every_token, w_gate, preferred_...]
    pallas_call x0 -> x1, Pallas kernels: none -> 212 us  [on_device(): pl.pallas_call(functools.partial(layer_kernel, Z, Y, Q, T, C, NF, NC), ou...]
    all_gather x3 -> x0, waiting for transfers between devices: 131 us -> none  [the longest x1 61.6 us: on_device(): act_all = lax.all_gather(activated, 'row', axis=0, tiled=True)]
    dot_general x4 -> x0, matrix products: 55.5 us -> none  [the longest x1 16.4 us: on_device(): jnp.dot(every_token, w_up, preferred_element_type=jnp.float32)]
    psum x1 -> x0, blocking collectives: 17.6 us -> none  [on_device(): sum_squares = lax.psum(partial_value, 'row')]
    concatenate x1 -> x0, other arithmetic: 5.26 us -> none  [on_device(): jnp.concatenate([jnp.dot(every_token, w_gate, preferred_element_type=jnp....]
  transfers between devices with their start and end apart: 6 -> 0, of which waited for: 6 -> 0; matrix products, arithmetic and copies ran while one was open for 0% -> 0% of each run, Pallas kernels for 0% -> 0%
where the time goes in v1:
time: 213 us
  Pallas kernels  212 us (100%)
    pallas_call x1, Pallas kernels, on_device(): pl.pallas_call(functools.partial(layer_kernel, Z, Y, Q, T, C, NF, NC), ou...  212 us

profile of v1, /device:TPU:1, one launch (start us, length us, event | category | flops | bytes accessed | tf_op | source)
XLA Modules:
  0.0 213.3 jit_solution(11994352468835363194)
XLA Ops:
  0.0 211.6 %shard_map.73 = bf16[64,2048]{1,0:T(8,128)(2,1)} custom-call(bf16[32,4096]{1,0:T(8,128)(2,1)} %attn.1, bf16[4096,2048]{1,0:T(8,128)(2,1)} %w_out.1, bf16[64,2048]{1,0:T(8,128)(2,1)} %resid.1, f32[1,2048]{1,0:T(1,128)} %bitcast.1, bf16[2048,6656]{1,0:T(8,128)(2,1)} %w_gate.1, bf16[2048,6656]{1,0:T(8,128)(2,1)} %w_up.1, bf16[6656,2048]{1,0:T(8,128)(2,1)} %w_down.1), custom_call_target="tpu_custom_call" | custom-call | tf_op jit(solution)/shard_map/pallas_call | solution.py:289
  211.6 1.7 copy.9

commit v2 on v1

--- a/solution.py
+++ b/solution.py
@@ -11,6 +11,7 @@
 F32, BF16 = jnp.float32, jnp.bfloat16
 epsilon = 1e-05
 SLOTS = 3
+CORES = 2
 
 
 def chunk_of(hidden):
@@ -30,16 +31,19 @@
     out,
     wo_buf, wg_buf, wu_buf,
     feat, ysend, yrecv, zrecv, act,
-    acc, normed, stream, dsend, drecv1, drecv2, sq_send, sq_recv,
+    acc, normed, stream, dsend, core_recv1, x_recv1, core_recv2, x_recv2, squares, sq_recv, scale,
     wo_sem, wg_sem, wu_sem, wd_sem,
     f_zs, f_zr, f_ys, f_yr,
     r_ys, r_yr, r_zs, r_zr,
     a_zs, a_zr, a_ys, a_yr,
-    p_s, p_r, d_s, d_r, q_s, q_r, n_s, n_r,
+    pc_s, pc_r, px_s, px_r, dc_s, dc_r, dx_s, dx_r,
+    q_s, q_r, qc_s, qc_r, nc_s, nc_r, nx_s, nx_r,
 ):
     n = Z * Y
     row, col = lax.axis_index("row"), lax.axis_index("col")
     z, y = row // Y, lax.rem(row, Y)
+    x, core = col // CORES, lax.rem(col, CORES)
+    X = Q // CORES
     tokens, width = normed.shape
     TB = tokens // Q
 
@@ -106,26 +110,32 @@
             for d in range(1, Y)
         ]
 
-    def reduce_cols(recv, s_sem, r_sem):
+    def reduce_cols(core_recv, x_recv, cs, cr, xs, xr):
         for r in range(n):
             at = ((r % Y) * Z + r // Y) * T
-            dsend[r * T : (r + 1) * T] = acc[at : at + T].astype(BF16)
-        copies = []
-        for d in range(1, Q):
-            peer = lax.rem(col + d, Q)
-            copies.append(
-                to_col(
-                    dsend.at[pl.ds(pl.multiple_of(peer * TB, TB), TB)],
-                    recv.at[d - 1], s_sem.at[d - 1], r_sem.at[d - 1], peer,
-                )
-            )
-        for copy in copies:
-            copy.start()
-        total = dsend[pl.ds(pl.multiple_of(col * TB, TB), TB)].astype(F32)
-        for copy in copies:
+            q, off = (r * T) // TB, (r * T) % TB
+            dsend[q % CORES, q // CORES, off : off + T] = acc[at : at + T].astype(BF16)
+        order = [lax.rem(x + d, X) for d in (*range(1, X), 0)]
+        core_copies = [
+            to_col(dsend.at[1 - core, to], core_recv.at[i], cs.at[i], cr.at[i], x * CORES + 1 - core)
+            for i, to in enumerate(order)
+        ]
+        for copy in core_copies:
+            copy.start()
+        x_copies = []
+        for i, to in enumerate(order):
+            core_copies[i].wait_recv()
+            total = dsend[core, to].astype(F32) + core_recv[i].astype(F32)
+            if i < X - 1:
+                dsend[core, to] = total.astype(BF16)
+                copy = to_col(dsend.at[core, to], x_recv.at[i], xs.at[i], xr.at[i], to * CORES + core)
+                copy.start()
+                x_copies.append(copy)
+        for copy in core_copies:
+            copy.wait_send()
+        for i, copy in enumerate(x_copies):
             copy.wait()
-        for d in range(Q - 1):
-            total = total + recv[d].astype(F32)
+            total = total + x_recv[i].astype(F32)
         return total
 
     for f in range(NF):
@@ -160,34 +170,62 @@
     def _(c):
         load_wd(c).start()
 
-    stream_now = (resid[...].astype(F32) + reduce_cols(drecv1, p_s, p_r)).astype(BF16)
+    stream_now = (resid[...].astype(F32) + reduce_cols(core_recv1, x_recv1, pc_s, pc_r, px_s, px_r)).astype(BF16)
     stream[...] = stream_now
     stream_f = stream_now.astype(F32)
 
-    sq_send[...] = jnp.broadcast_to(jnp.sum(stream_f * stream_f, axis=1, keepdims=True), sq_send.shape)
-    copies = [
-        to_row(sq_send, sq_recv.at[d - 1], q_s.at[d - 1], q_r.at[d - 1], lax.rem(row + d, n))
-        for d in range(1, n)
+    def block(q):
+        return pl.ds(pl.multiple_of(q * TB, TB), TB)
+
+    own = block(col)
+    normed[own] = (stream_f * gain[...]).astype(BF16)
+
+    def share(at, i):
+        return to_col(normed.at[at], normed.at[at], nc_s.at[i], nc_r.at[i], x * CORES + 1 - core)
+
+    x_copies = [
+        to_col(normed.at[own], normed.at[own], nx_s.at[d - 1], nx_r.at[d - 1], lax.rem(x + d, X) * CORES + core)
+        for d in range(1, X)
     ]
-    for copy in copies:
+    shares = [share(own, 0)]
+    for copy in x_copies + shares:
+        copy.start()
+    squares[own] = jnp.broadcast_to(jnp.sum(stream_f * stream_f, axis=1, keepdims=True), (TB, squares.shape[1]))
+    sq_copies = [
+        to_col(squares.at[own], squares.at[own], qc_s.at[d - 1], qc_r.at[d - 1], lax.rem(col + d, Q))
+        for d in range(1, Q)
+    ]
+    for copy in sq_copies:
         copy.start()
     acc[...] = jnp.zeros_like(acc)
-    for copy in copies:
+    for d in range(1, X):
+        x_copies[d - 1].wait_recv()
+        shares.append(share(block(lax.rem(x + X - d, X) * CORES + core), d))
+        shares[d].start()
+    for copy in sq_copies:
         copy.wait()
-    squares = sq_send[...]
-    for d in range(n - 1):
-        squares = squares + sq_recv[d]
-    scale = lax.rsqrt(squares[:, :1] / (width * n) + epsilon)
-    own = pl.ds(pl.multiple_of(col * TB, TB), TB)
-    normed[own] = (stream[...].astype(F32) * scale * gain[...]).astype(BF16)
-    copies = [
-        to_col(normed.at[own], normed.at[own], n_s.at[d - 1], n_r.at[d - 1], lax.rem(col + d, Q))
-        for d in range(1, Q)
-    ]
-    for copy in copies:
+
+    def send_squares():
+        copies = []
+        for d in range(1, n):
+            peer = lax.rem(row + d, n)
+            src = squares.at[pl.ds(pl.multiple_of(peer * T, T), T)]
+            copies.append(to_row(src, sq_recv.at[d - 1], q_s.at[d - 1], q_r.at[d - 1], peer))
+        return copies
+
+    for copy in send_squares():
         copy.start()
-    for copy in copies:
+    for copy in x_copies:
+        copy.wait_send()
+    for copy in shares:
         copy.wait()
+
+    def find_scale():
+        total = squares[pl.ds(pl.multiple_of(row * T, T), T)]
+        for d, copy in enumerate(send_squares()):
+            copy.wait()
+            total = total + sq_recv[d]
+        scale[...] = lax.rsqrt(total / (width * n) + epsilon)
 
     def reduce_y(c):
         return [
@@ -233,7 +271,8 @@
         total = ysend[c, y, z].astype(F32)
         for d in range(Z - 1):
             total = total + zrecv[c, d].astype(F32)
-        gate, up = total[:, :C], total[:, C:]
+        by = scale[:, :1]
+        gate, up = total[:, :C] * by, total[:, C:] * by
         act[c, y, z] = (gate / (1.0 + jnp.exp(-gate)) * up).astype(BF16)
         for copy in gather_z(act, c, a_zs, a_zr):
             copy.start()
@@ -256,17 +295,21 @@
         def _():
             load_wd(c + NF).start()
 
-    stages = ((0, multiply), (2, add_y), (3, activate), (4, pass_on), (5, project_down))
-
-    @pl.loop(0, NC + 5)
+    stages = ((0, multiply), (2, add_y), (3, activate), (4, pass_on), (6, project_down))
+
+    @pl.loop(0, NC + 6)
     def _(t):
+        @pl.when(t == 2)
+        def _():
+            find_scale()
+
         for lag, stage in stages:
 
             @pl.when((t >= lag) & (t < NC + lag))
             def _():
                 stage(t - lag)
 
-    out[...] = (stream[...].astype(F32) + reduce_cols(drecv2, d_s, d_r)).astype(out.dtype)
+    out[...] = (stream[...].astype(F32) + reduce_cols(core_recv2, x_recv2, dc_s, dc_r, dx_s, dx_r)).astype(out.dtype)
 
 
 def on_device(Z, Y, Q, attn_in, w_out, resid, norm_gain, w_gate, w_up, w_down):
@@ -275,6 +318,7 @@
     width, hidden = w_gate.shape
     tokens = T * n
     TB = tokens // Q
+    X = Q // CORES
     C = chunk_of(hidden)
     NF, NC = features // C, hidden // C
     dma = pltpu.SemaphoreType.DMA
@@ -303,16 +347,20 @@
             pltpu.VMEM((tokens, width), F32),
             pltpu.VMEM((tokens, width), BF16),
             pltpu.VMEM((TB, width), BF16),
-            pltpu.VMEM((tokens, width), BF16),
-            pltpu.VMEM((Q - 1, TB, width), BF16),
-            pltpu.VMEM((Q - 1, TB, width), BF16),
-            pltpu.VMEM((TB, 128), F32),
-            pltpu.VMEM((n - 1, TB, 128), F32),
+            pltpu.VMEM((CORES, X, TB, width), BF16),
+            pltpu.VMEM((X, TB, width), BF16),
+            pltpu.VMEM((X - 1, TB, width), BF16),
+            pltpu.VMEM((X, TB, width), BF16),
+            pltpu.VMEM((X - 1, TB, width), BF16),
+            pltpu.VMEM((tokens, 128), F32),
+            pltpu.VMEM((n - 1, T, 128), F32),
+            pltpu.VMEM((T, 128), F32),
             dma((NF,)), dma((SLOTS,)), dma((SLOTS,)), dma((NF,)),
             *pairs(NF, Z - 1), *pairs(NF, Y - 1),
             *pairs(NC, Y - 1), *pairs(NC, Z - 1),
             *pairs(NC, Z - 1), *pairs(NC, Y - 1),
-            *both(Q - 1), *both(Q - 1), *both(n - 1), *both(Q - 1),
+            *both(X), *both(X - 1), *both(X), *both(X - 1),
+            *both(n - 1), *both(Q - 1), *both(X), *both(X - 1),
         ],
         compiler_params=pltpu.CompilerParams(
             collective_id=0, has_side_effects=True, vmem_limit_bytes=60 * 2**20

time: 213 us -> 200 us (0.939)
  Pallas kernels: 212 us -> 198 us
    pallas_call x1, Pallas kernels: 212 us -> 198 us  [on_device(): pl.pallas_call(functools.partial(layer_kernel, Z, Y, Q, T, C, NF, NC), ou...]
where the time goes in v2:
time: 200 us; the launch traced here: 199 us
  Pallas kernels  198 us (99%)
    pallas_call x1, Pallas kernels, on_device(): pl.pallas_call(functools.partial(layer_kernel, Z, Y, Q, T, C, NF, NC), ou...  198 us

profile of v2, /device:TPU:1, one launch (start us, length us, event | category | flops | bytes accessed | tf_op | source)
XLA Modules:
  0.0 199.4 jit_solution(13284538652741464518)
XLA Ops:
  0.0 197.7 %shard_map.73 = bf16[64,2048]{1,0:T(8,128)(2,1)} custom-call(bf16[32,4096]{1,0:T(8,128)(2,1)} %attn.1, bf16[4096,2048]{1,0:T(8,128)(2,1)} %w_out.1, bf16[64,2048]{1,0:T(8,128)(2,1)} %resid.1, f32[1,2048]{1,0:T(1,128)} %bitcast.1, bf16[2048,6656]{1,0:T(8,128)(2,1)} %w_gate.1, bf16[2048,6656]{1,0:T(8,128)(2,1)} %w_up.1, bf16[6656,2048]{1,0:T(8,128)(2,1)} %w_down.1), custom_call_target="tpu_custom_call" | custom-call | tf_op jit(solution)/shard_map/pallas_call | solution.py:333
  197.7 1.7 copy.9

commit v3 on v2

--- a/solution.py
+++ b/solution.py
@@ -10,12 +10,12 @@
 MESH = pl.DeviceIdType.MESH
 F32, BF16 = jnp.float32, jnp.bfloat16
 epsilon = 1e-05
-SLOTS = 3
+SLOTS = 6
 CORES = 2
 
 
 def chunk_of(hidden):
-    return max(c for c in range(128, 513, 128) if hidden % c == 0)
+    return max(c for c in range(128, 257, 128) if hidden % c == 0)
 
 
 def grid_of(rows):
@@ -295,9 +295,9 @@
         def _():
             load_wd(c + NF).start()
 
-    stages = ((0, multiply), (2, add_y), (3, activate), (4, pass_on), (6, project_down))
-
-    @pl.loop(0, NC + 6)
+    stages = ((0, multiply), (3, add_y), (5, activate), (7, pass_on), (11, project_down))
+
+    @pl.loop(0, NC + stages[-1][0])
     def _(t):
         @pl.when(t == 2)
         def _():

time: 200 us -> 204 us (1.020)
  Pallas kernels: 198 us -> 203 us
    pallas_call x1, Pallas kernels: 198 us -> 203 us  [on_device(): pl.pallas_call(functools.partial(layer_kernel, Z, Y, Q, T, C, NF, NC), ou...]
where the time goes in v3:
time: 204 us
  Pallas kernels  203 us (100%)
    pallas_call x1, Pallas kernels, on_device(): pl.pallas_call(functools.partial(layer_kernel, Z, Y, Q, T, C, NF, NC), ou...  203 us

profile of v3, /device:TPU:1, one launch (start us, length us, event | category | flops | bytes accessed | tf_op | source)
XLA Modules:
  0.0 204.3 jit_solution(1655575532625997587)
XLA Ops:
  0.0 202.7 %shard_map.73 = bf16[64,2048]{1,0:T(8,128)(2,1)} custom-call(bf16[32,4096]{1,0:T(8,128)(2,1)} %attn.1, bf16[4096,2048]{1,0:T(8,128)(2,1)} %w_out.1, bf16[64,2048]{1,0:T(8,128)(2,1)} %resid.1, f32[1,2048]{1,0:T(1,128)} %bitcast.1, bf16[2048,6656]{1,0:T(8,128)(2,1)} %w_gate.1, bf16[2048,6656]{1,0:T(8,128)(2,1)} %w_up.1, bf16[6656,2048]{1,0:T(8,128)(2,1)} %w_down.1), custom_call_target="tpu_custom_call" | custom-call | tf_op jit(solution)/shard_map/pallas_call | solution.py:333
  202.7 1.7 copy.9
